TPU v7x, 256 devices: a whole 4x4x8 slice. The times are simulated.
256 devices in a mesh: var: 8 (over x, y_lo), space: 32 (over y_hi, z, core).
Axes of the slice: x: 4, y: 4 (y_hi: 2, y_lo: 2; y = y_hi * 2 + y_lo), z: 8, core: 2. Of those that a mesh axis runs over, the one named last changes fastest.
Arguments:
- order_field: float32 [128, 3, 1024, 1024], P('var', None, 'space'), may hold values from -1 to 1
- solute: float32 [3, 1024, 1024], P(None, 'space'), may hold values from 0.05 to 0.95
- active: int32 [32, 64], P(None, 'var'), may hold values from 0 to 1, as said below
Outputs:
- new_order: float32 [128, 3, 1024, 1024], P('var', None, 'space')
- new_solute: float32 [3, 1024, 1024], P(None, 'space')
Inputs may be any that keep to these rules, and one draw needn't show every extreme that they name: On every tile, each index of var holds at least 1 and at most 4 active blocks among its 8; in every draw some tile and index of var hold exactly 4.
All inputs are finite; a program needn't handle non-finite values.
Results may differ from a plain program's by a relative error of at most 0.00005.
Values sent between devices are 32-bit elements; how exact they have to be, the bound alone decides.
A program may use at most 128 MiB of HBM per device.

v0:
```python
import jax
import jax.numpy as jnp
from jax import lax
from jax.sharding import PartitionSpec as P


def with_halo(value, sides, width):
    for axis, dim in sides:
        peers, length = (lax.axis_size(axis), value.shape[dim])
        up = [(i, (i + 1) % peers) for i in range(peers)]
        down = [(j, i) for i, j in up]
        last = lax.slice_in_dim(value, length - width, length, axis=dim)
        leading = lax.slice_in_dim(value, 0, width, axis=dim)
        before = lax.ppermute(last, axis, up)
        after = lax.ppermute(leading, axis, down)
        value = jnp.concatenate([before, value, after], axis=dim)
    return value


def laplace_rows(extended):
    center = extended[..., 1:-1, :]
    summed = extended[..., 2:, :] + extended[..., :-2, :]
    summed = summed + jnp.roll(center, 1, axis=-1) + jnp.roll(center, -1, axis=-1)
    above_plane = jnp.concatenate([center[..., 1:, :, :], center[..., -1:, :, :]], axis=-3)
    below_plane = jnp.concatenate([center[..., :1, :, :], center[..., :-1, :, :]], axis=-3)
    return summed + above_plane + below_plane - 6.0 * center


def order_update(live_eta, sum_squares, solute, lap_eta):
    shifted = solute - 0.05
    change = -0.5 * shifted * shifted * live_eta + live_eta * live_eta * live_eta
    change = change + 0.4 * live_eta * (sum_squares - live_eta * live_eta) - 2.0 * lap_eta
    return live_eta - 0.01 * change


def chemical(solute_rows, square_rows, lap_solute):
    middle = solute_rows - 0.5
    shifted = solute_rows - 0.05
    upper_gap = solute_rows - 0.95
    potential = -2.0 * middle + 9.88 * middle**3 + 2.0 * shifted**3 + 2.0 * upper_gap**3
    return potential - 0.5 * shifted * square_rows - lap_solute


def shards(order_field, solute, active):
    tile_index = lax.axis_index("space")
    local_variants = order_field.shape[0]
    block_count = active.shape[1]
    block_size = local_variants // block_count
    tiles_iota = jnp.arange(active.shape[0], dtype=jnp.int32)
    picked = (tiles_iota == tile_index).astype(jnp.int32)
    own_mask = jnp.sum(active * picked[:, None], axis=0)
    weight_vector = jnp.repeat(own_mask.astype(jnp.float32), block_size)
    live_terms = order_field * weight_vector[:, None, None, None]
    extended = with_halo(live_terms, (("space", 2),), 1)
    partial_sum = jnp.sum(live_terms * live_terms, axis=0)
    sum_squares = lax.psum(partial_sum, "var")
    updated = order_update(live_terms, sum_squares, solute, laplace_rows(extended))
    new_order = updated * weight_vector[:, None, None, None]
    near_solute = with_halo(solute, (("space", 1),), 1)
    potential_core = chemical(solute, sum_squares, laplace_rows(near_solute))
    potential = with_halo(potential_core, (("space", 1),), 1)
    new_solute = solute + 0.01 * laplace_rows(potential)
    return (new_order, new_solute)


def solution(mesh):
    return jax.shard_map(
        shards,
        mesh=mesh,
        in_specs=(P("var", None, "space", None), P(None, "space", None), P(None, "var")),
        out_specs=(P("var", None, "space", None), P(None, "space", None)),
        check_vma=False,
    )
```

profile of v0, /device:TPU:1, one launch (start us, length us, event | category | flops | bytes accessed | tf_op | source)
XLA Modules:
  0.0 142.2 jit_solution(15473535257818549671)
XLA Ops:
  7.2 1.6 %fusion.47 = (f32[3,1,1024]{2,1,0:T(1,128)}, f32[3,1,1024]{2,1,0:T(1,128)S(1)}) fusion(f32[3,32,1024]{2,1,0:T(8,128)} %param.4), kind=kLoop, calls=%fused_computation.62 | loop fusion | bytes 49152 | tf_op jit(solution)/shard_map/slice | solution.py:13
  8.8 3.2 %collective-permute-start.2 = (f32[3,1,1024]{2,1,0:T(1,128)}, f32[3,1,1024]{2,1,0:T(1,128)S(1)}, u32[]{:S(2)}, u32[]{:S(2)}) collective-permute-start(f32[3,1,1024]{2,1,0:T(1,128)} %get-tuple-element.36), channel_id=1, source_target_pairs={{1,0},{2,1},{3,2},{4,3},{5,4},{6,5},{7,6},{8,7},{9,8},{10,9},{11,1... | collective-permute-start | bytes 36872 | tf_op jit(solution)/shard_map/ppermute | solution.py:15
  12.0 0.8 multiply_reduce_fusion.1
  12.9 0.1 mul.114
  13.0 11.0 %multiply_reduce_fusion = (f32[3,32,1024]{2,1,0:T(8,128)}, f32[16,3,32,1024]{3,0,2,1:T(8,128)}) fusion(f32[16]{0:T(128)S(1)} %mul.114, f32[16,3,32,1024]{3,2,1,0:T(8,128)} %param.3), kind=kLoop, calls=%fused_computation.15 | loop fusion | flops 4620288 | bytes 12976192 | tf_op jit(solution)/shard_map/reduce_sum | solution.py:55
  24.1 2.0 %fusion.37 = (f32[16,3,1,1024]{3,0,2,1:T(8,128)}, f32[16,3,1,1024]{3,0,2,1:T(8,128)}) fusion(f32[16,3,32,1024]{3,0,2,1:T(8,128)} %get-tuple-element.5), kind=kLoop, calls=%fused_computation.52 | loop fusion | bytes 786432 | tf_op jit(solution)/shard_map/slice | solution.py:13
  26.0 6.2 %collective-permute-start = (f32[16,3,1,1024]{3,0,2,1:T(8,128)}, f32[16,3,1,1024]{3,0,2,1:T(8,128)}, u32[]{:S(2)}, u32[]{:S(2)}) collective-permute-start(f32[16,3,1,1024]{3,0,2,1:T(8,128)} %get-tuple-element.14), channel_id=1, source_target_pairs={{1,0},{2,1},{3,2},{4,3},{5,4},{6,5},{7,6},{8,7},{9,8},{10,9},{11,1... | collective-permute-start | bytes 589832 | tf_op jit(solution)/shard_map/ppermute | solution.py:15
  32.2 0.8 fusion.44
  33.0 1.0 fusion.45
  34.1 2.8 %fusion.36 = (f32[16,3,32,1]{3,0,2,1:T(8,128)}, f32[16,3,32,1]{3,0,2,1:T(8,128)}) fusion(f32[16,3,32,1024]{3,0,2,1:T(8,128)} %get-tuple-element.5), kind=kLoop, calls=%fused_computation.51 | loop fusion | bytes 24576 | tf_op jit(solution)/shard_map/jit(_roll_static)/slice | solution.py:23
  36.9 2.3 %fusion.33 = (f32[16,1,32,1024]{3,0,2,1:T(8,128)}, f32[16,1,32,1024]{3,0,2,1:T(8,128)}) fusion(f32[16,3,32,1024]{3,0,2,1:T(8,128)S(1)} %copy-done), kind=kLoop, calls=%fused_computation.48 | loop fusion | bytes 8388608 | tf_op jit(solution)/shard_map/slice | solution.py:25
  39.2 4.2 %fusion.34 = (f32[16,2,32,1024]{3,0,2,1:T(8,128)}, f32[16,2,32,1024]{3,0,2,1:T(8,128)}) fusion(f32[16,3,32,1024]{3,0,2,1:T(8,128)S(1)} %copy-done), kind=kLoop, calls=%fused_computation.49 | loop fusion | bytes 16777216 | tf_op jit(solution)/shard_map/slice | solution.py:25
  43.4 6.7 %fusion.35 = (f32[16,3,32,1023]{3,0,2,1:T(8,128)}, f32[16,3,32,1023]{3,0,2,1:T(8,128)}) fusion(f32[16,3,32,1024]{3,0,2,1:T(8,128)S(1)} %copy-done), kind=kLoop, calls=%fused_computation.50 | loop fusion | bytes 25141248 | tf_op jit(solution)/shard_map/jit(_roll_static)/slice | solution.py:23
  50.1 0.7 fusion.43
  50.8 0.1 fusion.46
  50.9 51.5 %all-reduce.2.cloned.1.call-done = f32[3,32,1024]{2,1,0:T(8,128)} async-done(((f32[3,32,1024]{2,1,0:T(8,128)}), f32[3,32,1024]{2,1,0:T(8,128)}) %all-reduce.2.cloned.1.call-update) | async-done | bytes 393232 | tf_op jit(solution)/shard_map/psum | solution.py:56
  102.4 2.0 %fusion.16 = f32[3,32,1024]{2,1,0:T(8,128)S(1)} fusion(f32[3,32,1024]{2,1,0:T(8,128)S(1)} %copy-done.2, f32[3,1,1024]{2,1,0:T(1,128)S(1)} %collective-permute-done.3, f32[3,1,1024]{2,1,0:T(1,128)S(1)} %collective-permute-done.2, f32[3,32,1023]{2,1,0:T(8,128)} %get-tuple-element.33, f32[3,32,1]{2,1,0:T(8,128)S(1)} %get-tuple-element.35, ...), kind=kLoop, calls=%fused_computation.25 | loop fusion | flops 3244032 | bytes 2777088 | tf_op jit(solution)/shard_map/sub | solution.py:41
  104.6 0.2 fusion.40
  104.7 6.0 %collective-permute-start.4 = (f32[3,1,1024]{2,1,0:T(1,128)S(1)}, f32[3,1,1024]{2,1,0:T(1,128)S(1)}, u32[]{:S(2)}, u32[]{:S(2)}) collective-permute-start(f32[3,1,1024]{2,1,0:T(1,128)S(1)} %get-tuple-element.26), channel_id=1, source_target_pairs={{1,0},{2,1},{3,2},{4,3},{5,4},{6,5},{7,6},{8,7},{9,8},{10,9},{11,1... | collective-permute-start | bytes 36872 | tf_op jit(solution)/shard_map/ppermute | solution.py:15
  110.8 1.5 %collective-permute-start.5 = (f32[3,1,1024]{2,1,0:T(1,128)S(1)}, f32[3,1,1024]{2,1,0:T(1,128)S(1)}, u32[]{:S(2)}, u32[]{:S(2)}) collective-permute-start(f32[3,1,1024]{2,1,0:T(1,128)S(1)} %get-tuple-element.27), channel_id=1, source_target_pairs={{0,1},{1,2},{2,3},{3,4},{4,5},{5,6},{6,7},{7,8},{8,9},{9,10},{10,1... | collective-permute-start | bytes 36872 | tf_op jit(solution)/shard_map/ppermute | solution.py:14
  112.3 1.0 collective-permute-done.4
  113.3 1.1 fusion.26
  114.4 14.6 %fusion.10 = f32[16,3,32,1024]{3,0,2,1:T(8,128)S(1)} fusion(f32[16,3,32,1024]{3,0,2,1:T(8,128)} %get-tuple-element.5, f32[16,3,1,1024]{3,0,2,1:T(8,128)} %collective-permute-done.1, f32[16,3,1,1024]{3,0,2,1:T(8,128)} %collective-permute-done, f32[16,3,32,1023]{3,0,2,1:T(8,128)} %get-tuple-element.11, f32[16,3,32,1]{3,0,2,1:T(8,128)S(1)} %copy-done.5, ...), kind=kLoop, calls=%fused_computation.11 | loop fusion | flops 39321600 | bytes 38928448 | tf_op jit(solution)/shard_map/mul | solution.py:58
  129.0 6.3 %copy.6 = f32[16,3,32,1024]{3,2,1,0:T(8,128)} copy(f32[16,3,32,1024]{3,0,2,1:T(8,128)S(1)} %fusion.10) | data formatting | bytes 12582912
  (28 shorter events, 0.3 us)
Async XLA Ops:
  7.2 95.2 %all-reduce.2.cloned.1.call-start = ((), (), s32[]{:S(2)}) async-start(), calls=%async_computation | async-start | bytes 786432 | tf_op jit(solution)/shard_map/psum | solution.py:56
  8.8 42.1 %collective-permute-start.2 = (f32[3,1,1024]{2,1,0:T(1,128)}, f32[3,1,1024]{2,1,0:T(1,128)S(1)}, u32[]{:S(2)}, u32[]{:S(2)}) collective-permute-start(f32[3,1,1024]{2,1,0:T(1,128)} %get-tuple-element.36), channel_id=1, source_target_pairs={{1,0},{2,1},{3,2},{4,3},{5,4},{6,5},{7,6},{8,7},{9,8},{10,9},{11,1... | collective-permute-start | bytes 36872 | tf_op jit(solution)/shard_map/ppermute | solution.py:15
  12.0 38.8 %collective-permute-start.3 = (f32[3,1,1024]{2,1,0:T(1,128)S(1)}, f32[3,1,1024]{2,1,0:T(1,128)S(1)}, u32[]{:S(2)}, u32[]{:S(2)}) collective-permute-start(f32[3,1,1024]{2,1,0:T(1,128)S(1)} %get-tuple-element.37), channel_id=1, source_target_pairs={{0,1},{1,2},{2,3},{3,4},{4,5},{5,6},{6,7},{7,8},{8,9},{9,10},{10,1... | collective-permute-start | bytes 36872 | tf_op jit(solution)/shard_map/ppermute | solution.py:14
  13.0 19.2 %copy-start.2 = (f32[3,32,1024]{2,1,0:T(8,128)S(1)}, f32[3,32,1024]{2,1,0:T(8,128)}, u32[]{:S(2)}) copy-start(f32[3,32,1024]{2,1,0:T(8,128)} %param.4) | copy-start | bytes 1179652
  24.0 12.9 %copy-start = (f32[16,3,32,1024]{3,0,2,1:T(8,128)S(1)}, f32[16,3,32,1024]{3,0,2,1:T(8,128)}, u32[]{:S(2)}) copy-start(f32[16,3,32,1024]{3,0,2,1:T(8,128)} %get-tuple-element.5) | copy-start | bytes 18874372
  26.0 88.4 %collective-permute-start = (f32[16,3,1,1024]{3,0,2,1:T(8,128)}, f32[16,3,1,1024]{3,0,2,1:T(8,128)}, u32[]{:S(2)}, u32[]{:S(2)}) collective-permute-start(f32[16,3,1,1024]{3,0,2,1:T(8,128)} %get-tuple-element.14), channel_id=1, source_target_pairs={{1,0},{2,1},{3,2},{4,3},{5,4},{6,5},{7,6},{8,7},{9,8},{10,9},{11,1... | collective-permute-start | bytes 589832 | tf_op jit(solution)/shard_map/ppermute | solution.py:15
  32.2 82.2 %collective-permute-start.1 = (f32[16,3,1,1024]{3,0,2,1:T(8,128)}, f32[16,3,1,1024]{3,0,2,1:T(8,128)}, u32[]{:S(2)}, u32[]{:S(2)}) collective-permute-start(f32[16,3,1,1024]{3,0,2,1:T(8,128)} %get-tuple-element.15), channel_id=1, source_target_pairs={{0,1},{1,2},{2,3},{3,4},{4,5},{5,6},{6,7},{7,8},{8,9},{9,10},{10,1... | collective-permute-start | bytes 589832 | tf_op jit(solution)/shard_map/ppermute | solution.py:14
  50.1 64.3 %copy-start.3 = (f32[16,1,32,1024]{3,0,2,1:T(8,128)S(1)}, f32[16,1,32,1024]{3,0,2,1:T(8,128)}, u32[]{:S(2)}) copy-start(f32[16,1,32,1024]{3,0,2,1:T(8,128)} %get-tuple-element.6) | copy-start | bytes 6291460
  50.1 64.3 %copy-start.4 = (f32[16,3,32,1]{3,0,2,1:T(8,128)S(1)}, f32[16,3,32,1]{3,0,2,1:T(8,128)}, u32[]{:S(2)}) copy-start(f32[16,3,32,1]{3,0,2,1:T(8,128)} %get-tuple-element.12) | copy-start | bytes 18436
  102.4 12.0 %copy-start.1 = (f32[16,3,32,1023]{3,0,2,1:T(8,128)S(1)}, f32[16,3,32,1023]{3,0,2,1:T(8,128)}, u32[]{:S(2)}) copy-start(f32[16,3,32,1023]{3,0,2,1:T(8,128)} %get-tuple-element.10) | copy-start | bytes 18855940
  102.4 12.0 %copy-start.5 = (f32[16,3,32,1]{3,0,2,1:T(8,128)S(1)}, f32[16,3,32,1]{3,0,2,1:T(8,128)}, u32[]{:S(2)}) copy-start(f32[16,3,32,1]{3,0,2,1:T(8,128)} %get-tuple-element.13) | copy-start | bytes 18436
  104.7 8.6 %collective-permute-start.4 = (f32[3,1,1024]{2,1,0:T(1,128)S(1)}, f32[3,1,1024]{2,1,0:T(1,128)S(1)}, u32[]{:S(2)}, u32[]{:S(2)}) collective-permute-start(f32[3,1,1024]{2,1,0:T(1,128)S(1)} %get-tuple-element.26), channel_id=1, source_target_pairs={{1,0},{2,1},{3,2},{4,3},{5,4},{6,5},{7,6},{8,7},{9,8},{10,9},{11,1... | collective-permute-start | bytes 36872 | tf_op jit(solution)/shard_map/ppermute | solution.py:15
  110.8 2.5 %collective-permute-start.5 = (f32[3,1,1024]{2,1,0:T(1,128)S(1)}, f32[3,1,1024]{2,1,0:T(1,128)S(1)}, u32[]{:S(2)}, u32[]{:S(2)}) collective-permute-start(f32[3,1,1024]{2,1,0:T(1,128)S(1)} %get-tuple-element.27), channel_id=1, source_target_pairs={{0,1},{1,2},{2,3},{3,4},{4,5},{5,6},{6,7},{7,8},{8,9},{9,10},{10,1... | collective-permute-start | bytes 36872 | tf_op jit(solution)/shard_map/ppermute | solution.py:14
Sparse Core Ops, SparseCore 0:
  24.2 78.1 all-reduce.1
where the time goes:
time: 145 us; the launch traced here: 142 us
  waiting for transfers between devices  52.6 us (36%)
  other arithmetic  29.5 us (20%)
  local copies, waits for them, and re-layouts  29 us (20%)
  starting transfers between devices  17 us (12%)
  between operations  14.1 us (10%)
    psum x1, waiting for transfers between devices, shards(): sum_squares = lax.psum(partial_sum, 'var')  51.5 us
    ppermute x3, starting transfers between devices, with_halo(): after = lax.ppermute(leading, axis, down)  15.5 us
    mul x1, other arithmetic, shards(): new_order = updated * weight_vector[:, None, None, None]  14.6 us
    reduce_sum x1, other arithmetic, shards(): partial_sum = jnp.sum(live_terms * live_terms, axis=0)  11 us
    slice x6, local copies, waits for them, and re-layouts, laplace_rows(): jnp.roll(center, -1, axis=-1)  10.9 us
    unnamed x13, local copies, waits for them, and re-layouts  6.37 us
    slice x3, local copies, waits for them, and re-layouts, laplace_rows(): center[..., :-1, :, :]  5.06 us
    slice x3, local copies, waits for them, and re-layouts, with_halo(): leading = lax.slice_in_dim(value, 0, width, axis=dim)  3.53 us
  transfers between devices with their start and end apart: 7, of which 2 were waited for; matrix products, arithmetic and copies ran while one was open for 25% of the time, Pallas kernels for 0%

commit v1 on v0

v1 whole, which is shorter than its diff:
```python
import functools

import jax
import jax.numpy as jnp
from jax import lax
from jax.experimental import pallas as pl
from jax.experimental.pallas import tpu as pltpu
from jax.sharding import PartitionSpec as P

MESH = pl.DeviceIdType.MESH
F32 = jnp.float32
PLANES, ROWS, COLS, LANES = 3, 32, 1024, 128
VARIANTS, BLOCKS, BV, KMAX = 16, 8, 2, 4
SLOTS = KMAX * BV
GROUP, TILES = 8, 32
PEERS = ((1, 0), (0, 1), (3, 0), (2, 1), (1, 1), (2, 0), (3, 1))


def tile_blocks(active_ref, tile):
    flags = [active_ref[tile, b] for b in range(BLOCKS)]
    blocks = [jnp.int32(0)] * KMAX
    rank = jnp.int32(0)
    for b in range(BLOCKS):
        for k in range(KMAX):
            hit = jnp.where(rank == k, flags[b], 0)
            blocks[k] = blocks[k] + b * hit
        rank = rank + flags[b]
    weights = [jnp.where(rank > k, 1.0, 0.0).astype(F32) for k in range(KMAX)]
    return blocks, weights


def rows_sum(value):
    row = lax.broadcasted_iota(jnp.int32, value.shape, 0)
    before = jnp.where(row == 0, 0.0, pltpu.roll(value, 1, 0))
    after = jnp.where(row == value.shape[0] - 1, 0.0, pltpu.roll(value, value.shape[0] - 1, 0))
    return before + after


def cells_sum(value):
    return pltpu.roll(value, 1, 1) + pltpu.roll(value, value.shape[1] - 1, 1)


def plane_sum(planes, z):
    return planes[min(z + 1, PLANES - 1)] + planes[max(z - 1, 0)]


def bulk(value):
    middle = value - 0.5
    shifted = value - 0.05
    gap = value - 0.95
    return (-2.0 * middle + 9.88 * middle * middle * middle
            + 2.0 * shifted * shifted * shifted + 2.0 * gap * gap * gap)


def exchange(order, solute, active, base, slope, squares, quiet, held, edge_quiet, edge_held, edge_squares,
             field0, field1, field2, part, landed, row_out, row_in, edge_out,
             load_sem, solute_sem, row_send, row_recv, sum_send, sum_recv, all_send, all_recv, edge_send, edge_recv):
    v, tile = lax.axis_index("var"), lax.axis_index("space")
    x, y = v // 2, v % 2
    below, above = lax.rem(tile + TILES - 1, TILES), lax.rem(tile + 1, TILES)
    sides = (below, above)
    peers = [lax.rem(x + dx, 4) * 2 + (y + dy - 2 * y * dy) for dx, dy in PEERS]
    fields = (field0, field1, field2)

    loads = [pltpu.make_async_copy(order.at[:, z], fields[z], load_sem.at[z]) for z in range(PLANES)]
    for copy in loads:
        copy.start()
    solute_load = pltpu.make_async_copy(solute, held, solute_sem)
    solute_load.start()

    barrier = pltpu.get_barrier_semaphore()
    for peer in peers:
        pl.semaphore_signal(barrier, inc=1, device_id=(peer, tile), device_id_type=MESH)
    for side in sides:
        for d in range(GROUP):
            pl.semaphore_signal(barrier, inc=1, device_id=(lax.rem(v + d, GROUP), side), device_id_type=MESH)

    blocks, weights = tile_blocks(active, tile)
    side_blocks = [tile_blocks(active, side)[0] for side in sides]

    waiting = []
    sums = []
    for z in range(PLANES):
        loads[z].wait()
        total = jnp.zeros((ROWS, COLS), F32)
        for k in range(KMAX):
            for i in range(BV):
                one = fields[z][blocks[k] * BV + i]
                total = total + one * one * weights[k]
        for p in range(GROUP):
            part[z, p] = total[:, p * LANES:(p + 1) * LANES]
        if z == 0:
            pl.semaphore_wait(barrier, GROUP - 1 + 2 * GROUP)
        for d, peer in enumerate(peers):
            copy = pltpu.make_async_remote_copy(
                part.at[z, peer], landed.at[z, d], sum_send.at[z, d], sum_recv.at[z, d],
                device_id=(peer, tile), device_id_type=MESH)
            copy.start()
            sums.append(copy)

    solute_load.wait()
    row_copies = []
    for s, side in enumerate(sides):
        edge = 0 if s == 0 else ROWS - 1
        for k in range(KMAX):
            block = side_blocks[s][k]
            weight = active[tile, block].astype(F32)
            for i in range(BV):
                slot = k * BV + i
                for z in range(PLANES):
                    row_out[s, z * SLOTS + slot:z * SLOTS + slot + 1, :] = (
                        fields[z][block * BV + i, edge:edge + 1, :] * weight)
        first = 0 if s == 0 else ROWS - 2
        for z in range(PLANES):
            row_out[s, 24 + 2 * z:26 + 2 * z, :] = held[z, first:first + 2, :]
        row_out[s, 30:32, :] = jnp.zeros((2, COLS), F32)
        copy = pltpu.make_async_remote_copy(
            row_out.at[s], row_in.at[1 - s], row_send.at[s], row_recv.at[1 - s],
            device_id=(v, side), device_id_type=MESH)
        copy.start()
        row_copies.append(copy)

    def local(slot, block, weight, i):
        ones = [fields[z][block * BV + i] for z in range(PLANES)]
        for z in range(PLANES):
            one = ones[z]
            shifted = held[z] - 0.05
            near = rows_sum(one) + cells_sum(one) + plane_sum(ones, z)
            value = one * (0.88 + 0.005 * (shifted * shifted) - 0.006 * (one * one)) + 0.02 * near
            base[slot, z] = value * weight
            slope[slot, z] = one * (0.004 * weight)

    def reduce_plane(z):
        total = part[z, v]
        for d in range(GROUP - 1):
            sums[z * (GROUP - 1) + d].wait_recv()
            total = total + landed[z, d]
        squares[z, v] = total
        edge_out[0, z:z + 1, :] = total[0:1, :]
        edge_out[1, z:z + 1, :] = total[ROWS - 1:ROWS, :]
        for d, peer in enumerate(peers):
            copy = pltpu.make_async_remote_copy(
                squares.at[z, v], squares.at[z, v], all_send.at[z, d], all_recv.at[z, d],
                device_id=(peer, tile), device_id_type=MESH)
            copy.start()
            gathers.append(copy)

    gathers = []
    edge_out[0, 3:8, :] = jnp.zeros((5, LANES), F32)
    edge_out[1, 3:8, :] = jnp.zeros((5, LANES), F32)
    for k in range(KMAX):
        for i in range(BV):
            local(k * BV + i, blocks[k], weights[k], i)
    reduce_plane(0)
    solutes = [held[z] for z in range(PLANES)]
    for z in range(PLANES):
        value = solutes[z]
        quiet[z] = bulk(value) + 6.0 * value - rows_sum(value) - cells_sum(value) - plane_sum(solutes, z)
    reduce_plane(1)
    reduce_plane(2)
    edges = []
    for s, side in enumerate(sides):
        for d in range(GROUP):
            copy = pltpu.make_async_remote_copy(
                edge_out.at[s], edge_squares.at[1 - s, v], edge_send.at[s, d], edge_recv.at[1 - s, d],
                device_id=(lax.rem(v + d, GROUP), side), device_id_type=MESH)
            copy.start()
            edges.append(copy)

    for copy in row_copies:
        copy.wait_recv()
    for s in range(2):
        row = 0 if s == 0 else ROWS - 1
        for k in range(KMAX):
            for i in range(BV):
                slot = k * BV + i
                for z in range(PLANES):
                    base[slot, z, row:row + 1, :] = base[slot, z, row:row + 1, :] + (
                        row_in[s, z * SLOTS + slot:z * SLOTS + slot + 1, :] * (0.02 * weights[k]))
        near_row, far_row = (1, 0) if s == 0 else (0, 1)
        nears = [row_in[s, 24 + 2 * z + near_row:25 + 2 * z + near_row, :] for z in range(PLANES)]
        for z in range(PLANES):
            far = row_in[s, 24 + 2 * z + far_row:25 + 2 * z + far_row, :]
            quiet[z, row:row + 1, :] = quiet[z, row:row + 1, :] - nears[z]
            around = far + held[z, row:row + 1, :] + cells_sum(nears[z]) + plane_sum(nears, z)
            edge_quiet[s, z:z + 1, :] = bulk(nears[z]) + 6.0 * nears[z] - around
            edge_held[s, z:z + 1, :] = nears[z]
        edge_quiet[s, 3:8, :] = jnp.zeros((5, COLS), F32)
        edge_held[s, 3:8, :] = jnp.zeros((5, COLS), F32)

    for copy in gathers:
        copy.wait_recv()
    for copy in edges:
        copy.wait_recv()
    for copy in sums + gathers + edges + row_copies:
        copy.wait_send()


def finish(active, base, slope, squares, quiet, held, edge_quiet, edge_held, edge_squares, new_order, new_solute,
           blank, stage, solute_stage, order_sem, solute_sem):
    tile = lax.axis_index("space")
    blank[...] = jnp.zeros(blank.shape, F32)
    flags = [active[tile, b] for b in range(BLOCKS)]
    for b in range(BLOCKS):
        @pl.when(flags[b] == 0)
        def _():
            pltpu.make_async_copy(blank, new_order.at[pl.ds(b * BV, BV)], order_sem.at[b]).start()
    rank = jnp.int32(0)
    for b in range(BLOCKS):
        @pl.when(flags[b] != 0)
        def _(rank=rank):
            for i in range(BV):
                for z in range(PLANES):
                    for p in range(GROUP):
                        cut = slice(p * LANES, (p + 1) * LANES)
                        stage[rank, i, z, :, cut] = (
                            base[rank * BV + i, z, :, cut] - slope[rank * BV + i, z, :, cut] * squares[z, p])
            pltpu.make_async_copy(stage.at[rank], new_order.at[pl.ds(b * BV, BV)], order_sem.at[b]).start()
        rank = rank + flags[b]

    pots = []
    for z in range(PLANES):
        total = jnp.concatenate([squares[z, p] for p in range(GROUP)], axis=1)
        pots.append(quiet[z] - 0.5 * (held[z] - 0.05) * total)
    ends = []
    for s in range(2):
        total = jnp.concatenate([edge_squares[s, p] for p in range(GROUP)], axis=1)
        ends.append(edge_quiet[s] - 0.5 * (edge_held[s] - 0.05) * total)
    row = lax.broadcasted_iota(jnp.int32, (ROWS, COLS), 0)
    for z in range(PLANES):
        value = pots[z]
        before = jnp.where(row == 0, jnp.broadcast_to(ends[0][z:z + 1, :], (ROWS, COLS)), pltpu.roll(value, 1, 0))
        after = jnp.where(row == ROWS - 1, jnp.broadcast_to(ends[1][z:z + 1, :], (ROWS, COLS)),
                          pltpu.roll(value, ROWS - 1, 0))
        lap = before + after + cells_sum(value) + plane_sum(pots, z) - 6.0 * value
        solute_stage[z] = held[z] + 0.01 * lap
    out = pltpu.make_async_copy(solute_stage, new_solute, solute_sem)
    out.start()
    for b in range(BLOCKS):
        pltpu.make_async_copy(blank, new_order.at[pl.ds(b * BV, BV)], order_sem.at[b]).wait()
    out.wait()


def shards(order, solute, active):
    vmem = pl.BlockSpec(memory_space=pltpu.VMEM)
    smem = pl.BlockSpec(memory_space=pltpu.SMEM)
    anywhere = pl.BlockSpec(memory_space=pl.ANY)
    dma = pltpu.SemaphoreType.DMA
    handed = [
        (SLOTS, PLANES, ROWS, COLS),
        (SLOTS, PLANES, ROWS, COLS),
        (PLANES, GROUP, ROWS, LANES),
        (PLANES, ROWS, COLS),
        (PLANES, ROWS, COLS),
        (2, 8, COLS),
        (2, 8, COLS),
        (2, GROUP, 8, LANES),
    ]
    results = pl.pallas_call(
        exchange,
        out_shape=[pltpu.VMEM(shape, F32) for shape in handed],
        in_specs=[anywhere, anywhere, smem],
        out_specs=[vmem] * len(handed),
        scratch_shapes=[
            pltpu.VMEM((VARIANTS, ROWS, COLS), F32),
            pltpu.VMEM((VARIANTS, ROWS, COLS), F32),
            pltpu.VMEM((VARIANTS, ROWS, COLS), F32),
            pltpu.VMEM((PLANES, GROUP, ROWS, LANES), F32),
            pltpu.VMEM((PLANES, GROUP - 1, ROWS, LANES), F32),
            pltpu.VMEM((2, 32, COLS), F32),
            pltpu.VMEM((2, 32, COLS), F32),
            pltpu.VMEM((2, 8, LANES), F32),
            dma((PLANES,)),
            dma,
            dma((2,)),
            dma((2,)),
            dma((PLANES, GROUP - 1)),
            dma((PLANES, GROUP - 1)),
            dma((PLANES, GROUP - 1)),
            dma((PLANES, GROUP - 1)),
            dma((2, GROUP)),
            dma((2, GROUP)),
        ],
        compiler_params=pltpu.CompilerParams(
            collective_id=0, has_side_effects=True, vmem_limit_bytes=32 << 20),
        name="exchange",
    )(order, solute, active)
    return pl.pallas_call(
        finish,
        out_shape=[
            jax.ShapeDtypeStruct(order.shape, F32),
            jax.ShapeDtypeStruct(solute.shape, F32),
        ],
        in_specs=[smem] + [vmem] * len(handed),
        out_specs=[anywhere, anywhere],
        scratch_shapes=[
            pltpu.VMEM((BV, PLANES, ROWS, COLS), F32),
            pltpu.VMEM((KMAX, BV, PLANES, ROWS, COLS), F32),
            pltpu.VMEM((PLANES, ROWS, COLS), F32),
            dma((BLOCKS,)),
            dma,
        ],
        compiler_params=pltpu.CompilerParams(vmem_limit_bytes=32 << 20),
        name="finish",
    )(active, *results)


def solution(mesh):
    return jax.shard_map(
        shards,
        mesh=mesh,
        in_specs=(P("var", None, "space", None), P(None, "space", None), P(None, "var")),
        out_specs=(P("var", None, "space", None), P(None, "space", None)),
        check_vma=False,
    )
```

time: 145 us -> 35 us (0.24); the launches traced: 142 us -> 34.8 us
  waiting for transfers between devices: 52.6 us -> 0 us
  Pallas kernels: 0 us -> 29.6 us
  other arithmetic: 29.5 us -> 0 us
  local copies, waits for them, and re-layouts: 29 us -> 4.54 us
  starting transfers between devices: 17 us -> 0 us
  between operations: 14.1 us -> 0.64 us
    psum x1 -> x0, waiting for transfers between devices: 51.5 us -> none  [shards(): sum_squares = lax.psum(partial_sum, 'var')]
    pallas_call x0 -> x2, Pallas kernels: none -> 29.6 us  [the longest x1 25.9 us: shards(): pl.pallas_call(exchange, out_shape=[pltpu.VMEM(shape, F32) for shape in h...]
    slice x15 -> x0, local copies, waits for them, and re-layouts: 22.5 us -> none  [the longest x6 10.9 us: laplace_rows(): jnp.roll(center, -1, axis=-1)]
    ppermute x6 -> x0, starting transfers between devices: 16.9 us -> none  [the longest x3 15.5 us: with_halo(): after = lax.ppermute(leading, axis, down)]
    mul x1 -> x0, other arithmetic: 14.6 us -> none  [shards(): new_order = updated * weight_vector[:, None, None, None]]
    reduce_sum x2 -> x0, other arithmetic: 11.8 us -> none  [the longest x1 11 us: shards(): partial_sum = jnp.sum(live_terms * live_terms, axis=0)]
    sub x1 -> x0, other arithmetic: 2.04 us -> none  [chemical(): return potential - 0.5 * shifted * square_rows - lap_solute]
    unnamed x13 -> x5, local copies, waits for them, and re-layouts: 6.37 us -> 4.54 us
  transfers between devices with their start and end apart: 7 -> 0, of which waited for: 2 -> 0; matrix products, arithmetic and copies ran while one was open for 25% -> 0% of each run, Pallas kernels for 0% -> 0%
where the time goes in v1:
time: 35 us; the launch traced here: 34.8 us
  Pallas kernels  29.6 us (85%)
  local copies, waits for them, and re-layouts  4.54 us (13%)
  between operations  0.64 us (2%)
    pallas_call x1, Pallas kernels, shards(): pl.pallas_call(exchange, out_shape=[pltpu.VMEM(shape, F32) for shape in h...  25.9 us
    unnamed x5, local copies, waits for them, and re-layouts  4.54 us
    pallas_call x1, Pallas kernels, shards(): pl.pallas_call(finish, out_shape=[jax.ShapeDtypeStruct(order.shape, F32),...  3.7 us

profile of v1, /device:TPU:1, one launch (start us, length us, event | category | flops | bytes accessed | tf_op | source)
XLA Modules:
  0.0 34.8 jit_solution(5108949989924205004)
XLA Ops:
  0.6 0.8 %copy.6.active = s32[32,8]{1,0:T(8,128)S(1)} copy(s32[32,8]{0,1:T(8,128)} %param.5) | data formatting | bytes 2048 | tf_op args[2]
  1.4 0.0 copy-start
  1.4 2.8 %copy-done = f32[16,3,32,1024]{3,2,1,0:T(8,128)S(1)} copy-done((f32[16,3,32,1024]{3,2,1,0:T(8,128)S(1)}, f32[16,3,32,1024]{3,2,1,0:T(8,128)}, u32[]{:S(2)}) %copy-start) | copy-done | bytes 6291480
  4.2 0.0 copy-start.1
  4.2 1.0 %copy-done.1 = f32[3,32,1024]{2,1,0:T(8,128)S(1)} copy-done((f32[3,32,1024]{2,1,0:T(8,128)S(1)}, f32[3,32,1024]{2,1,0:T(8,128)}, u32[]{:S(2)}) %copy-start.1) | copy-done | bytes 393240
  5.2 25.9 %exchange.1 = (f32[8,3,32,1024]{3,2,1,0:T(8,128)S(1)}, f32[8,3,32,1024]{3,2,1,0:T(8,128)S(1)}, f32[3,8,32,128]{3,2,1,0:T(8,128)S(1)}, f32[3,32,1024]{2,1,0:T(8,1...) custom-call(f32[16,3,32,1024]{3,2,1,0:T(8,128)S(1)} %copy-done, ...), custom_call_target="tpu_custom_call" | custom-call | tf_op jit(solution)/shard_map/exchange/pallas_call | solution.py:259
  31.1 3.7 %finish.1 = (f32[16,3,32,1024]{3,2,1,0:T(8,128)}, f32[3,32,1024]{2,1,0:T(8,128)}) custom-call(s32[32,8]{1,0:T(8,128)S(1)} %copy.6.active, f32[8,3,32,1024]{3,2,1,0:T(8,128)S(1)} %get-tuple-element.10.base, f32[8,3,32,1024]{3,2,1,0:T(8,128)S(1)} %get-tuple-element.11.slope, f32[3,8,32,128]{3,2,1,0:T(8,128)S(1)} %get-tuple-element.12.squares, ...), custom_call_target="tpu_custom_call" | custom-call | tf_op jit(solution)/shard_map/finish/pallas_call | solution.py:288
Async XLA Ops:
  1.4 2.8 %copy-start = (f32[16,3,32,1024]{3,2,1,0:T(8,128)S(1)}, f32[16,3,32,1024]{3,2,1,0:T(8,128)}, u32[]{:S(2)}) copy-start(f32[16,3,32,1024]{3,2,1,0:T(8,128)} %order.1) | copy-start | bytes 18874372
  4.2 1.0 %copy-start.1 = (f32[3,32,1024]{2,1,0:T(8,128)S(1)}, f32[3,32,1024]{2,1,0:T(8,128)}, u32[]{:S(2)}) copy-start(f32[3,32,1024]{2,1,0:T(8,128)} %solute.1) | copy-start | bytes 1179652

commit v2 on v1

v2 whole, which is shorter than its diff:
```python
import functools

import jax
import jax.numpy as jnp
from jax import lax
from jax.experimental import pallas as pl
from jax.experimental.pallas import tpu as pltpu
from jax.sharding import PartitionSpec as P

MESH = pl.DeviceIdType.MESH
F32 = jnp.float32
PLANES, ROWS, COLS, LANES = 3, 32, 1024, 128
VARIANTS, BLOCKS, BV, KMAX = 16, 8, 2, 4
SLOTS = KMAX * BV
GROUP, TILES = 8, 32
SUB, GROUPS = 8, 4
PIECES = (0, 3, 1, 2)
PEERS = ((1, 0), (0, 1), (3, 0), (2, 1), (1, 1), (2, 0), (3, 1))


def tile_blocks(active_ref, tile):
    flags = [active_ref[b, tile] for b in range(BLOCKS)]
    blocks = [jnp.int32(0)] * KMAX
    rank = jnp.int32(0)
    for b in range(BLOCKS):
        for k in range(KMAX):
            hit = jnp.where(rank == k, flags[b], 0)
            blocks[k] = blocks[k] + b * hit
        rank = rank + flags[b]
    weights = [jnp.where(rank > k, 1.0, 0.0).astype(F32) for k in range(KMAX)]
    return blocks, weights


def rows_sum(value):
    row = lax.broadcasted_iota(jnp.int32, value.shape, 0)
    before = jnp.where(row == 0, 0.0, pltpu.roll(value, 1, 0))
    after = jnp.where(row == value.shape[0] - 1, 0.0, pltpu.roll(value, value.shape[0] - 1, 0))
    return before + after


def cells_sum(value):
    return pltpu.roll(value, 1, 1) + pltpu.roll(value, value.shape[1] - 1, 1)


def plane_sum(planes, z):
    return planes[min(z + 1, PLANES - 1)] + planes[max(z - 1, 0)]


def bulk(value):
    middle = value - 0.5
    shifted = value - 0.05
    gap = value - 0.95
    return (-2.0 * middle + 9.88 * middle * middle * middle
            + 2.0 * shifted * shifted * shifted + 2.0 * gap * gap * gap)


def exchange(order, solute, active_hbm, base, slope, squares, quiet, held, edge_quiet, edge_held, edge_squares,
             field0, field1, field2, field3, part, landed, row_out, row_in, edge_out,
             active, active_sem, load_sem, solute_sem, near_sem, row_send, row_recv,
             sum_send, sum_recv, all_send, all_recv, edge_send, edge_recv):
    v, tile = lax.axis_index("var"), lax.axis_index("space")
    x, y = v // 2, v % 2
    below, above = lax.rem(tile + TILES - 1, TILES), lax.rem(tile + 1, TILES)
    sides = (below, above)
    peers = [lax.rem(x + dx, 4) * 2 + (y + dy - 2 * y * dy) for dx, dy in PEERS]
    fields = (field0, field1, field2, field3)

    active_load = pltpu.make_async_copy(active_hbm, active, active_sem)
    active_load.start()
    loads = {}
    for g in PIECES:
        loads[g] = pltpu.make_async_copy(order.at[:, :, pl.ds(g * SUB, SUB)], fields[g], load_sem.at[g])
        loads[g].start()
    solute_load = pltpu.make_async_copy(solute, held, solute_sem)
    solute_load.start()

    barrier = pltpu.get_barrier_semaphore()
    for peer in peers:
        pl.semaphore_signal(barrier, inc=1, device_id=(peer, tile), device_id_type=MESH)
    for d in range(GROUP):
        pl.semaphore_signal(barrier, inc=1, device_id=(lax.rem(v + d, GROUP), below), device_id_type=MESH)

    active_load.wait()
    blocks, weights = tile_blocks(active, tile)
    side_blocks = [tile_blocks(active, side)[0] for side in sides]

    sums = {}
    gathers, edges, row_copies = [], [], []

    def send_sums(g):
        loads[g].wait()
        for z in range(PLANES):
            total = jnp.zeros((SUB, COLS), F32)
            for k in range(KMAX):
                for i in range(BV):
                    one = fields[g][blocks[k] * BV + i, z]
                    total = total + one * one * weights[k]
            for p in range(GROUP):
                part[g, p, z] = total[:, p * LANES:(p + 1) * LANES]
        if g == PIECES[0]:
            pl.semaphore_wait(barrier, GROUP - 1 + GROUP)
        for d, peer in enumerate(peers):
            sums[g, d] = pltpu.make_async_remote_copy(
                part.at[g, peer], landed.at[g, d], sum_send.at[g, d], sum_recv.at[g, d],
                device_id=(peer, tile), device_id_type=MESH)
            sums[g, d].start()

    def send_rows(s):
        g, edge = (0, 0) if s == 0 else (GROUPS - 1, SUB - 1)
        for k in range(KMAX):
            block = side_blocks[s][k]
            weight = active[block, tile].astype(F32)
            for i in range(BV):
                slot = k * BV + i
                for z in range(PLANES):
                    row_out[s, z * SLOTS + slot:z * SLOTS + slot + 1, :] = (
                        fields[g][block * BV + i, z, edge:edge + 1, :] * weight)
        first = 0 if s == 0 else ROWS - 2
        for z in range(PLANES):
            row_out[s, 24 + 2 * z:26 + 2 * z, :] = held[z, first:first + 2, :]
        row_out[s, 30:32, :] = jnp.zeros((2, COLS), F32)
        copy = pltpu.make_async_remote_copy(
            row_out.at[s], row_in.at[1 - s], row_send.at[s], row_recv.at[1 - s],
            device_id=(v, sides[s]), device_id_type=MESH)
        copy.start()
        row_copies.append(copy)

    def local(k):
        for i in range(BV):
            slot = k * BV + i
            ones = [jnp.concatenate([field[blocks[k] * BV + i, z] for field in fields], axis=0)
                    for z in range(PLANES)]
            for z in range(PLANES):
                one = ones[z]
                shifted = held[z] - 0.05
                near = rows_sum(one) + cells_sum(one) + plane_sum(ones, z)
                value = one * (0.88 + 0.005 * (shifted * shifted) - 0.006 * (one * one)) + 0.02 * near
                base[slot, z] = value * weights[k]
                slope[slot, z] = one * (0.004 * weights[k])

    def reduce(g):
        total = part[g, v]
        for d in range(GROUP - 1):
            sums[g, d].wait_recv()
            total = total + landed[g, d]
        squares[g, v] = total
        for d, peer in enumerate(peers):
            copy = pltpu.make_async_remote_copy(
                squares.at[g, v], squares.at[g, v], all_send.at[g, d], all_recv.at[g, d],
                device_id=(peer, tile), device_id_type=MESH)
            copy.start()
            gathers.append(copy)
        if g in (0, GROUPS - 1):
            s, edge = (0, 0) if g == 0 else (1, SUB - 1)
            for z in range(PLANES):
                edge_out[s, z:z + 1, :] = total[z, edge:edge + 1, :]
            edge_out[s, 3:8, :] = jnp.zeros((5, LANES), F32)

    def send_edges(s):
        for d in range(GROUP):
            copy = pltpu.make_async_remote_copy(
                edge_out.at[s], edge_squares.at[1 - s, v], edge_send.at[s, d], edge_recv.at[1 - s, d],
                device_id=(lax.rem(v + d, GROUP), sides[s]), device_id_type=MESH)
            copy.start()
            edges.append(copy)

    for g in PIECES:
        send_sums(g)
    for d in range(GROUP):
        pl.semaphore_signal(near_sem, inc=1, device_id=(lax.rem(v + d, GROUP), above), device_id_type=MESH)
    solute_load.wait()
    send_rows(1)
    local(0)
    local(1)
    reduce(PIECES[0])
    local(2)
    reduce(PIECES[1])
    pl.semaphore_wait(near_sem, GROUP)
    send_edges(0)
    send_edges(1)
    send_rows(0)
    reduce(PIECES[2])
    local(3)
    reduce(PIECES[3])

    solutes = [held[z] for z in range(PLANES)]
    for z in range(PLANES):
        value = solutes[z]
        quiet[z] = bulk(value) + 6.0 * value - rows_sum(value) - cells_sum(value) - plane_sum(solutes, z)

    for copy in row_copies:
        copy.wait_recv()
    for s in range(2):
        row = 0 if s == 0 else ROWS - 1
        for k in range(KMAX):
            for i in range(BV):
                slot = k * BV + i
                for z in range(PLANES):
                    base[slot, z, row:row + 1, :] = base[slot, z, row:row + 1, :] + (
                        row_in[s, z * SLOTS + slot:z * SLOTS + slot + 1, :] * (0.02 * weights[k]))
        near_row, far_row = (1, 0) if s == 0 else (0, 1)
        nears = [row_in[s, 24 + 2 * z + near_row:25 + 2 * z + near_row, :] for z in range(PLANES)]
        for z in range(PLANES):
            far = row_in[s, 24 + 2 * z + far_row:25 + 2 * z + far_row, :]
            quiet[z, row:row + 1, :] = quiet[z, row:row + 1, :] - nears[z]
            around = far + held[z, row:row + 1, :] + cells_sum(nears[z]) + plane_sum(nears, z)
            edge_quiet[s, z:z + 1, :] = bulk(nears[z]) + 6.0 * nears[z] - around
            edge_held[s, z:z + 1, :] = nears[z]
        edge_quiet[s, 3:8, :] = jnp.zeros((5, COLS), F32)
        edge_held[s, 3:8, :] = jnp.zeros((5, COLS), F32)

    for copy in gathers + edges:
        copy.wait_recv()
    for copy in list(sums.values()) + gathers + edges + row_copies:
        copy.wait_send()


def finish(active_hbm, base, slope, squares, quiet, held, edge_quiet, edge_held, edge_squares, new_order, new_solute,
           active, active_sem, blank, stage, solute_stage, order_sem, solute_sem):
    tile = lax.axis_index("space")
    active_load = pltpu.make_async_copy(active_hbm, active, active_sem)
    active_load.start()
    blank[...] = jnp.zeros(blank.shape, F32)
    active_load.wait()
    flags = [active[b, tile] for b in range(BLOCKS)]
    for b in range(BLOCKS):
        @pl.when(flags[b] == 0)
        def _():
            pltpu.make_async_copy(blank, new_order.at[pl.ds(b * BV, BV)], order_sem.at[b]).start()
    totals = [
        jnp.concatenate(
            [jnp.concatenate([squares[g, p, z] for p in range(GROUP)], axis=1) for g in range(GROUPS)], axis=0)
        for z in range(PLANES)
    ]
    rank = jnp.int32(0)
    for b in range(BLOCKS):
        @pl.when(flags[b] != 0)
        def _(rank=rank):
            for i in range(BV):
                for z in range(PLANES):
                    stage[rank, i, z] = base[rank * BV + i, z] - slope[rank * BV + i, z] * totals[z]
            pltpu.make_async_copy(stage.at[rank], new_order.at[pl.ds(b * BV, BV)], order_sem.at[b]).start()
        rank = rank + flags[b]

    pots = []
    for z in range(PLANES):
        pots.append(quiet[z] - 0.5 * (held[z] - 0.05) * totals[z])
    ends = []
    for s in range(2):
        total = jnp.concatenate([edge_squares[s, p] for p in range(GROUP)], axis=1)
        ends.append(edge_quiet[s] - 0.5 * (edge_held[s] - 0.05) * total)
    row = lax.broadcasted_iota(jnp.int32, (ROWS, COLS), 0)
    for z in range(PLANES):
        value = pots[z]
        before = jnp.where(row == 0, jnp.broadcast_to(ends[0][z:z + 1, :], (ROWS, COLS)), pltpu.roll(value, 1, 0))
        after = jnp.where(row == ROWS - 1, jnp.broadcast_to(ends[1][z:z + 1, :], (ROWS, COLS)),
                          pltpu.roll(value, ROWS - 1, 0))
        lap = before + after + cells_sum(value) + plane_sum(pots, z) - 6.0 * value
        solute_stage[z] = held[z] + 0.01 * lap
    out = pltpu.make_async_copy(solute_stage, new_solute, solute_sem)
    out.start()
    for b in range(BLOCKS):
        pltpu.make_async_copy(blank, new_order.at[pl.ds(b * BV, BV)], order_sem.at[b]).wait()
    out.wait()


def shards(order, solute, active):
    vmem = pl.BlockSpec(memory_space=pltpu.VMEM)
    hbm = pl.BlockSpec(memory_space=pltpu.HBM)
    dma = pltpu.SemaphoreType.DMA
    handed = [
        (SLOTS, PLANES, ROWS, COLS),
        (SLOTS, PLANES, ROWS, COLS),
        (GROUPS, GROUP, PLANES, SUB, LANES),
        (PLANES, ROWS, COLS),
        (PLANES, ROWS, COLS),
        (2, 8, COLS),
        (2, 8, COLS),
        (2, GROUP, 8, LANES),
    ]
    order, solute, flags = (
        pltpu.with_memory_space_constraint(value, pltpu.HBM) for value in (order, solute, active.T))
    results = pl.pallas_call(
        exchange,
        out_shape=[pltpu.VMEM(shape, F32) for shape in handed],
        in_specs=[hbm, hbm, hbm],
        out_specs=[vmem] * len(handed),
        scratch_shapes=[
            pltpu.VMEM((VARIANTS, PLANES, SUB, COLS), F32),
            pltpu.VMEM((VARIANTS, PLANES, SUB, COLS), F32),
            pltpu.VMEM((VARIANTS, PLANES, SUB, COLS), F32),
            pltpu.VMEM((VARIANTS, PLANES, SUB, COLS), F32),
            pltpu.VMEM((GROUPS, GROUP, PLANES, SUB, LANES), F32),
            pltpu.VMEM((GROUPS, GROUP - 1, PLANES, SUB, LANES), F32),
            pltpu.VMEM((2, 32, COLS), F32),
            pltpu.VMEM((2, 32, COLS), F32),
            pltpu.VMEM((2, 8, LANES), F32),
            pltpu.SMEM((BLOCKS, TILES), jnp.int32),
            dma,
            dma((GROUPS,)),
            dma,
            pltpu.SemaphoreType.REGULAR,
            dma((2,)),
            dma((2,)),
            dma((GROUPS, GROUP - 1)),
            dma((GROUPS, GROUP - 1)),
            dma((GROUPS, GROUP - 1)),
            dma((GROUPS, GROUP - 1)),
            dma((2, GROUP)),
            dma((2, GROUP)),
        ],
        compiler_params=pltpu.CompilerParams(
            collective_id=0, has_side_effects=True, vmem_limit_bytes=32 << 20),
        name="exchange",
    )(order, solute, flags)
    return pl.pallas_call(
        finish,
        out_shape=[
            jax.ShapeDtypeStruct(order.shape, F32),
            jax.ShapeDtypeStruct(solute.shape, F32),
        ],
        in_specs=[hbm] + [vmem] * len(handed),
        out_specs=[hbm, hbm],
        scratch_shapes=[
            pltpu.SMEM((BLOCKS, TILES), jnp.int32),
            dma,
            pltpu.VMEM((BV, PLANES, ROWS, COLS), F32),
            pltpu.VMEM((KMAX, BV, PLANES, ROWS, COLS), F32),
            pltpu.VMEM((PLANES, ROWS, COLS), F32),
            dma((BLOCKS,)),
            dma,
        ],
        compiler_params=pltpu.CompilerParams(vmem_limit_bytes=32 << 20),
        name="finish",
    )(flags, *results)


def solution(mesh):
    return jax.shard_map(
        shards,
        mesh=mesh,
        in_specs=(P("var", None, "space", None), P(None, "space", None), P(None, "var")),
        out_specs=(P("var", None, "space", None), P(None, "space", None)),
        check_vma=False,
    )
```

time: 35 us -> 24.8 us (0.71)
  Pallas kernels: 29.6 us -> 24 us
  local copies, waits for them, and re-layouts: 4.54 us -> 0 us
    pallas_call x1, Pallas kernels: 25.9 us -> 20.4 us  [shards(): pl.pallas_call(exchange, out_shape=[pltpu.VMEM(shape, F32) for shape in h...]
    unnamed x5 -> x0, local copies, waits for them, and re-layouts: 4.54 us -> none
where the time goes in v2:
time: 24.8 us; the launch traced here: 24.7 us
  Pallas kernels  24 us (97%)
  between operations  0.64 us (3%)
    pallas_call x1, Pallas kernels, shards(): pl.pallas_call(exchange, out_shape=[pltpu.VMEM(shape, F32) for shape in h...  20.4 us
    pallas_call x1, Pallas kernels, shards(): pl.pallas_call(finish, out_shape=[jax.ShapeDtypeStruct(order.shape, F32),...  3.59 us

profile of v2, /device:TPU:1, one launch (start us, length us, event | category | flops | bytes accessed | tf_op | source)
XLA Modules:
  0.0 24.7 jit_solution(9517646760101633940)
XLA Ops:
  0.6 20.4 %exchange.1 = (f32[8,3,32,1024]{3,2,1,0:T(8,128)S(1)}, f32[8,3,32,1024]{3,2,1,0:T(8,128)S(1)}, f32[4,8,3,8,128]{4,3,2,1,0:T(8,128)S(1)}, f32[3,32,1024]{2,1,0:T(...) custom-call(f32[16,3,32,1024]{3,2,1,0:T(8,128)} %order.1, ...), custom_call_target="tpu_custom_call" | custom-call | tf_op jit(solution)/shard_map/exchange/pallas_call | solution.py:283
  21.1 3.6 %finish.1 = (f32[16,3,32,1024]{3,2,1,0:T(8,128)}, f32[3,32,1024]{2,1,0:T(8,128)}) custom-call(s32[8,32]{1,0:T(8,128)} %bitcast.2, f32[8,3,32,1024]{3,2,1,0:T(8,128)S(1)} %get-tuple-element.10.base, f32[8,3,32,1024]{3,2,1,0:T(8,128)S(1)} %get-tuple-element.11.slope, f32[4,8,3,8,128]{4,3,2,1,0:T(8,128)S(1)} %get-tuple-element.12.squares, ...), custom_call_target="tpu_custom_call" | custom-call | tf_op jit(solution)/shard_map/finish/pallas_call | solution.py:316

commit v3 on v2

--- a/solution.py
+++ b/solution.py
@@ -13,8 +13,10 @@
 VARIANTS, BLOCKS, BV, KMAX = 16, 8, 2, 4
 SLOTS = KMAX * BV
 GROUP, TILES = 8, 32
+HALF = TILES // 2
 SUB, GROUPS = 8, 4
-PIECES = (0, 3, 1, 2)
+PIECES = (3, 0, 1, 2)
+ROUTES = ("x", "direct", "direct", "y")
 PEERS = ((1, 0), (0, 1), (3, 0), (2, 1), (1, 1), (2, 0), (3, 1))
 
 
@@ -56,7 +58,7 @@
 
 def exchange(order, solute, active_hbm, base, slope, squares, quiet, held, edge_quiet, edge_held, edge_squares,
              field0, field1, field2, field3, part, landed, row_out, row_in, edge_out,
-             active, active_sem, load_sem, solute_sem, near_sem, row_send, row_recv,
+             picked, scale, active, active_sem, load_sem, solute_sem, near_sem, row_send, row_recv,
              sum_send, sum_recv, all_send, all_recv, edge_send, edge_recv):
     v, tile = lax.axis_index("var"), lax.axis_index("space")
     x, y = v // 2, v % 2
@@ -74,18 +76,28 @@
     solute_load = pltpu.make_async_copy(solute, held, solute_sem)
     solute_load.start()
 
+    first = jnp.where(lax.rem(tile, HALF) == 0, 1, 0)
+    last = jnp.where(lax.rem(tile, HALF) == HALF - 1, 1, 0)
+
+    def report(semaphore, side):
+        for d in range(GROUP):
+            pl.semaphore_signal(semaphore, inc=1, device_id=(lax.rem(v + d, GROUP), side), device_id_type=MESH)
+
     barrier = pltpu.get_barrier_semaphore()
     for peer in peers:
         pl.semaphore_signal(barrier, inc=1, device_id=(peer, tile), device_id_type=MESH)
-    for d in range(GROUP):
-        pl.semaphore_signal(barrier, inc=1, device_id=(lax.rem(v + d, GROUP), below), device_id_type=MESH)
+    pl.when(last == 0)(lambda: report(barrier, above))
+    pl.when(first == 1)(lambda: report(barrier, below))
 
     active_load.wait()
     blocks, weights = tile_blocks(active, tile)
+    for k in range(KMAX):
+        picked[k] = blocks[k]
+        scale[k] = weights[k]
     side_blocks = [tile_blocks(active, side)[0] for side in sides]
 
     sums = {}
-    gathers, edges, row_copies = [], [], []
+    gathers, arrived, row_copies = {}, set(), []
 
     def send_sums(g):
         loads[g].wait()
@@ -98,14 +110,14 @@
             for p in range(GROUP):
                 part[g, p, z] = total[:, p * LANES:(p + 1) * LANES]
         if g == PIECES[0]:
-            pl.semaphore_wait(barrier, GROUP - 1 + GROUP)
+            pl.semaphore_wait(barrier, GROUP - 1 + GROUP * (1 - first + last))
         for d, peer in enumerate(peers):
             sums[g, d] = pltpu.make_async_remote_copy(
                 part.at[g, peer], landed.at[g, d], sum_send.at[g, d], sum_recv.at[g, d],
                 device_id=(peer, tile), device_id_type=MESH)
             sums[g, d].start()
 
-    def send_rows(s):
+    def stage_rows(s):
         g, edge = (0, 0) if s == 0 else (GROUPS - 1, SUB - 1)
         for k in range(KMAX):
             block = side_blocks[s][k]
@@ -119,24 +131,45 @@
         for z in range(PLANES):
             row_out[s, 24 + 2 * z:26 + 2 * z, :] = held[z, first:first + 2, :]
         row_out[s, 30:32, :] = jnp.zeros((2, COLS), F32)
-        copy = pltpu.make_async_remote_copy(
+        row_copies.append(pltpu.make_async_remote_copy(
             row_out.at[s], row_in.at[1 - s], row_send.at[s], row_recv.at[1 - s],
-            device_id=(v, sides[s]), device_id_type=MESH)
-        copy.start()
-        row_copies.append(copy)
-
-    def local(k):
+            device_id=(v, sides[s]), device_id_type=MESH))
+
+    def local(k, carry):
         for i in range(BV):
             slot = k * BV + i
-            ones = [jnp.concatenate([field[blocks[k] * BV + i, z] for field in fields], axis=0)
+            weight = scale[k]
+            ones = [jnp.concatenate([field[picked[k] * BV + i, z] for field in fields], axis=0)
                     for z in range(PLANES)]
             for z in range(PLANES):
                 one = ones[z]
                 shifted = held[z] - 0.05
                 near = rows_sum(one) + cells_sum(one) + plane_sum(ones, z)
                 value = one * (0.88 + 0.005 * (shifted * shifted) - 0.006 * (one * one)) + 0.02 * near
-                base[slot, z] = value * weights[k]
-                slope[slot, z] = one * (0.004 * weights[k])
+                base[slot, z] = value * weight
+                slope[slot, z] = one * (0.004 * weight)
+        return carry
+
+    def gather(g, d, chunk, peer):
+        gathers[g, d] = pltpu.make_async_remote_copy(
+            squares.at[g, chunk], squares.at[g, chunk], all_send.at[g, d], all_recv.at[g, d],
+            device_id=(peer, tile), device_id_type=MESH)
+        gathers[g, d].start()
+
+    def arrive(g, d):
+        gathers[g, d].wait_recv()
+        arrived.add((g, d))
+
+    def forward(g):
+        flip = PEERS.index((0, 1))
+        if ROUTES[g] == "y":
+            arrive(g, flip)
+        for dx in (2, 1, 3):
+            if ROUTES[g] == "y":
+                gather(g, PEERS.index((dx, 1)), peers[flip], peers[PEERS.index((dx, 0))])
+            elif ROUTES[g] == "x":
+                arrive(g, PEERS.index((dx, 0)))
+                gather(g, PEERS.index((dx, 1)), lax.rem(x + 4 - dx, 4) * 2 + y, peers[flip])
 
     def reduce(g):
         total = part[g, v]
@@ -144,44 +177,56 @@
             sums[g, d].wait_recv()
             total = total + landed[g, d]
         squares[g, v] = total
-        for d, peer in enumerate(peers):
-            copy = pltpu.make_async_remote_copy(
-                squares.at[g, v], squares.at[g, v], all_send.at[g, d], all_recv.at[g, d],
-                device_id=(peer, tile), device_id_type=MESH)
-            copy.start()
-            gathers.append(copy)
+        for d, (dx, dy) in enumerate(PEERS):
+            if ROUTES[g] == "direct" or dx == 0 or dy == 0:
+                gather(g, d, v, peers[d])
         if g in (0, GROUPS - 1):
             s, edge = (0, 0) if g == 0 else (1, SUB - 1)
             for z in range(PLANES):
                 edge_out[s, z:z + 1, :] = total[z, edge:edge + 1, :]
-            edge_out[s, 3:8, :] = jnp.zeros((5, LANES), F32)
-
-    def send_edges(s):
-        for d in range(GROUP):
-            copy = pltpu.make_async_remote_copy(
-                edge_out.at[s], edge_squares.at[1 - s, v], edge_send.at[s, d], edge_recv.at[1 - s, d],
-                device_id=(lax.rem(v + d, GROUP), sides[s]), device_id_type=MESH)
+
+    def start(copies):
+        for copy in copies:
             copy.start()
-            edges.append(copy)
+
+    edges = [
+        [pltpu.make_async_remote_copy(
+            edge_out.at[s, 0:PLANES], edge_squares.at[1 - s, v, 0:PLANES], edge_send.at[s, d], edge_recv.at[1 - s, d],
+            device_id=(lax.rem(v + d, GROUP), sides[s]), device_id_type=MESH) for d in range(GROUP)]
+        for s in range(2)
+    ]
 
     for g in PIECES:
         send_sums(g)
-    for d in range(GROUP):
-        pl.semaphore_signal(near_sem, inc=1, device_id=(lax.rem(v + d, GROUP), above), device_id_type=MESH)
+        if g == PIECES[0]:
+            pl.when(first == 0)(lambda: report(near_sem.at[1], below))
+            pl.when(last == 1)(lambda: report(near_sem.at[0], above))
     solute_load.wait()
-    send_rows(1)
-    local(0)
-    local(1)
+    stage_rows(0)
+    stage_rows(1)
+
+    pl.when(last == 0)(lambda: pl.semaphore_wait(near_sem.at[1], GROUP))
+    row_copies[1].start()
+    pl.when(first == 0)(lambda: row_copies[0].start())
+    lax.fori_loop(0, 1, local, 0)
     reduce(PIECES[0])
-    local(2)
+    start(edges[1])
     reduce(PIECES[1])
-    pl.semaphore_wait(near_sem, GROUP)
-    send_edges(0)
-    send_edges(1)
-    send_rows(0)
+    pl.when(first == 0)(lambda: start(edges[0]))
     reduce(PIECES[2])
-    local(3)
+    forward(PIECES[0])
     reduce(PIECES[3])
+    forward(PIECES[1])
+
+    @pl.when(first == 1)
+    def _():
+        pl.semaphore_wait(near_sem.at[0], GROUP)
+        start(edges[0])
+        row_copies[0].start()
+
+    lax.fori_loop(1, 2, local, 0)
+    forward(PIECES[2])
+    lax.fori_loop(2, 4, local, 0)
 
     solutes = [held[z] for z in range(PLANES)]
     for z in range(PLANES):
@@ -206,12 +251,14 @@
             around = far + held[z, row:row + 1, :] + cells_sum(nears[z]) + plane_sum(nears, z)
             edge_quiet[s, z:z + 1, :] = bulk(nears[z]) + 6.0 * nears[z] - around
             edge_held[s, z:z + 1, :] = nears[z]
-        edge_quiet[s, 3:8, :] = jnp.zeros((5, COLS), F32)
-        edge_held[s, 3:8, :] = jnp.zeros((5, COLS), F32)
-
-    for copy in gathers + edges:
+
+    edges = edges[0] + edges[1]
+    for place in gathers:
+        if place not in arrived:
+            gathers[place].wait_recv()
+    for copy in edges:
         copy.wait_recv()
-    for copy in list(sums.values()) + gathers + edges + row_copies:
+    for copy in list(sums.values()) + list(gathers.values()) + edges + row_copies:
         copy.wait_send()
 
 
@@ -222,33 +269,39 @@
     active_load.start()
     blank[...] = jnp.zeros(blank.shape, F32)
     active_load.wait()
-    flags = [active[b, tile] for b in range(BLOCKS)]
-    for b in range(BLOCKS):
-        @pl.when(flags[b] == 0)
+
+    def clear(b, carry):
+        @pl.when(active[b, tile] == 0)
         def _():
             pltpu.make_async_copy(blank, new_order.at[pl.ds(b * BV, BV)], order_sem.at[b]).start()
+        return carry
+
+    lax.fori_loop(0, BLOCKS, clear, 0)
     totals = [
         jnp.concatenate(
             [jnp.concatenate([squares[g, p, z] for p in range(GROUP)], axis=1) for g in range(GROUPS)], axis=0)
         for z in range(PLANES)
     ]
-    rank = jnp.int32(0)
-    for b in range(BLOCKS):
-        @pl.when(flags[b] != 0)
-        def _(rank=rank):
+
+    def update(b, rank):
+        flag = active[b, tile]
+
+        @pl.when(flag != 0)
+        def _():
             for i in range(BV):
                 for z in range(PLANES):
                     stage[rank, i, z] = base[rank * BV + i, z] - slope[rank * BV + i, z] * totals[z]
             pltpu.make_async_copy(stage.at[rank], new_order.at[pl.ds(b * BV, BV)], order_sem.at[b]).start()
-        rank = rank + flags[b]
-
+        return rank + flag
+
+    lax.fori_loop(0, BLOCKS, update, jnp.int32(0))
     pots = []
     for z in range(PLANES):
         pots.append(quiet[z] - 0.5 * (held[z] - 0.05) * totals[z])
     ends = []
     for s in range(2):
-        total = jnp.concatenate([edge_squares[s, p] for p in range(GROUP)], axis=1)
-        ends.append(edge_quiet[s] - 0.5 * (edge_held[s] - 0.05) * total)
+        total = jnp.concatenate([edge_squares[s, p, 0:PLANES] for p in range(GROUP)], axis=1)
+        ends.append(edge_quiet[s, 0:PLANES] - 0.5 * (edge_held[s, 0:PLANES] - 0.05) * total)
     row = lax.broadcasted_iota(jnp.int32, (ROWS, COLS), 0)
     for z in range(PLANES):
         value = pots[z]
@@ -295,11 +348,13 @@
             pltpu.VMEM((2, 32, COLS), F32),
             pltpu.VMEM((2, 32, COLS), F32),
             pltpu.VMEM((2, 8, LANES), F32),
+            pltpu.SMEM((KMAX,), jnp.int32),
+            pltpu.SMEM((KMAX,), F32),
             pltpu.SMEM((BLOCKS, TILES), jnp.int32),
             dma,
             dma((GROUPS,)),
             dma,
-            pltpu.SemaphoreType.REGULAR,
+            pltpu.SemaphoreType.REGULAR((2,)),
             dma((2,)),
             dma((2,)),
             dma((GROUPS, GROUP - 1)),

time: 24.8 us -> 23.3 us (0.940)
  the two profiles are of different devices: /device:TPU:1 before, /device:TPU:225 now
where the time goes in v3:
time: 23.3 us; the launch traced here: 23.2 us
  Pallas kernels  22.6 us (97%)
  between operations  0.64 us (3%)
    pallas_call x1, Pallas kernels, shards(): pl.pallas_call(exchange, out_shape=[pltpu.VMEM(shape, F32) for shape in h...  18.9 us
    pallas_call x1, Pallas kernels, shards(): pl.pallas_call(finish, out_shape=[jax.ShapeDtypeStruct(order.shape, F32),...  3.61 us

profile of v3, /device:TPU:225, one launch (start us, length us, event | category | flops | bytes accessed | tf_op | source)
XLA Modules:
  0.0 23.2 jit_solution(12449794916970918505)
XLA Ops:
  0.6 18.9 %exchange.1 = (f32[8,3,32,1024]{3,2,1,0:T(8,128)S(1)}, f32[8,3,32,1024]{3,2,1,0:T(8,128)S(1)}, f32[4,8,3,8,128]{4,3,2,1,0:T(8,128)S(1)}, f32[3,32,1024]{2,1,0:T(...) custom-call(f32[16,3,32,1024]{3,2,1,0:T(8,128)} %order.1, ...), custom_call_target="tpu_custom_call" | custom-call | tf_op jit(solution)/shard_map/exchange/pallas_call | solution.py:336
  19.6 3.6 %finish.1 = (f32[16,3,32,1024]{3,2,1,0:T(8,128)}, f32[3,32,1024]{2,1,0:T(8,128)}) custom-call(s32[8,32]{1,0:T(8,128)} %bitcast.2, f32[8,3,32,1024]{3,2,1,0:T(8,128)S(1)} %get-tuple-element.10.base, f32[8,3,32,1024]{3,2,1,0:T(8,128)S(1)} %get-tuple-element.11.slope, f32[4,8,3,8,128]{4,3,2,1,0:T(8,128)S(1)} %get-tuple-element.12.squares, ...), custom_call_target="tpu_custom_call" | custom-call | tf_op jit(solution)/shard_map/finish/pallas_call | solution.py:371

commit v4 on v3

--- a/solution.py
+++ b/solution.py
@@ -17,7 +17,7 @@
 SUB, GROUPS = 8, 4
 PIECES = (3, 0, 1, 2)
 ROUTES = ("x", "direct", "direct", "y")
-PEERS = ((1, 0), (0, 1), (3, 0), (2, 1), (1, 1), (2, 0), (3, 1))
+PEERS = ((2, 1), (1, 1), (3, 1), (2, 0), (0, 1), (1, 0), (3, 0))
 
 
 def tile_blocks(active_ref, tile):
@@ -57,6 +57,7 @@
 
 
 def exchange(order, solute, active_hbm, base, slope, squares, quiet, held, edge_quiet, edge_held, edge_squares,
+             blank, code,
              field0, field1, field2, field3, part, landed, row_out, row_in, edge_out,
              picked, scale, active, active_sem, load_sem, solute_sem, near_sem, row_send, row_recv,
              sum_send, sum_recv, all_send, all_recv, edge_send, edge_recv):
@@ -208,6 +209,11 @@
     pl.when(last == 0)(lambda: pl.semaphore_wait(near_sem.at[1], GROUP))
     row_copies[1].start()
     pl.when(first == 0)(lambda: row_copies[0].start())
+    blank[...] = jnp.zeros(blank.shape, F32)
+    bits = jnp.int32(0)
+    for b in range(BLOCKS):
+        bits = bits + active[b, tile] * (1 << b)
+    code[...] = jnp.full(code.shape, bits.astype(F32), F32)
     lax.fori_loop(0, 1, local, 0)
     reduce(PIECES[0])
     start(edges[1])
@@ -262,16 +268,15 @@
         copy.wait_send()
 
 
-def finish(active_hbm, base, slope, squares, quiet, held, edge_quiet, edge_held, edge_squares, new_order, new_solute,
-           active, active_sem, blank, stage, solute_stage, order_sem, solute_sem):
-    tile = lax.axis_index("space")
-    active_load = pltpu.make_async_copy(active_hbm, active, active_sem)
-    active_load.start()
-    blank[...] = jnp.zeros(blank.shape, F32)
-    active_load.wait()
+def finish(base, slope, squares, quiet, held, edge_quiet, edge_held, edge_squares, blank, code, new_order, new_solute,
+           stage, solute_stage, order_sem, solute_sem):
+    bits = jnp.max(code[...]).astype(jnp.int32)
+
+    def flag_of(b):
+        return lax.bitwise_and(lax.shift_right_logical(bits, b), 1)
 
     def clear(b, carry):
-        @pl.when(active[b, tile] == 0)
+        @pl.when(flag_of(b) == 0)
         def _():
             pltpu.make_async_copy(blank, new_order.at[pl.ds(b * BV, BV)], order_sem.at[b]).start()
         return carry
@@ -284,7 +289,7 @@
     ]
 
     def update(b, rank):
-        flag = active[b, tile]
+        flag = flag_of(b)
 
         @pl.when(flag != 0)
         def _():
@@ -330,6 +335,8 @@
         (2, 8, COLS),
         (2, 8, COLS),
         (2, GROUP, 8, LANES),
+        (BV, PLANES, ROWS, COLS),
+        (8, LANES),
     ]
     order, solute, flags = (
         pltpu.with_memory_space_constraint(value, pltpu.HBM) for value in (order, solute, active.T))
@@ -374,12 +381,9 @@
             jax.ShapeDtypeStruct(order.shape, F32),
             jax.ShapeDtypeStruct(solute.shape, F32),
         ],
-        in_specs=[hbm] + [vmem] * len(handed),
+        in_specs=[vmem] * len(handed),
         out_specs=[hbm, hbm],
         scratch_shapes=[
-            pltpu.SMEM((BLOCKS, TILES), jnp.int32),
-            dma,
-            pltpu.VMEM((BV, PLANES, ROWS, COLS), F32),
             pltpu.VMEM((KMAX, BV, PLANES, ROWS, COLS), F32),
             pltpu.VMEM((PLANES, ROWS, COLS), F32),
             dma((BLOCKS,)),
@@ -387,7 +391,7 @@
         ],
         compiler_params=pltpu.CompilerParams(vmem_limit_bytes=32 << 20),
         name="finish",
-    )(flags, *results)
+    )(*results)
 
 
 def solution(mesh):

time: 23.3 us -> 22.6 us (0.970)
  the two profiles are of different devices: /device:TPU:225 before, /device:TPU:2 now
where the time goes in v4:
time: 22.6 us; the launch traced here: 22.5 us
  Pallas kernels  21.9 us (97%)
  between operations  0.64 us (3%)
    pallas_call x1, Pallas kernels, shards(): pl.pallas_call(exchange, out_shape=[pltpu.VMEM(shape, F32) for shape in h...  18.9 us
    pallas_call x1, Pallas kernels, shards(): pl.pallas_call(finish, out_shape=[jax.ShapeDtypeStruct(order.shape, F32),...  2.97 us

profile of v4, /device:TPU:2, one launch (start us, length us, event | category | flops | bytes accessed | tf_op | source)
XLA Modules:
  0.0 22.5 jit_solution(10125666156557689680)
XLA Ops:
  0.6 18.9 %exchange.1 = (f32[8,3,32,1024]{3,2,1,0:T(8,128)S(1)}, f32[8,3,32,1024]{3,2,1,0:T(8,128)S(1)}, f32[4,8,3,8,128]{4,3,2,1,0:T(8,128)S(1)}, f32[3,32,1024]{2,1,0:T(...) custom-call(f32[16,3,32,1024]{3,2,1,0:T(8,128)} %order.1, ...), custom_call_target="tpu_custom_call" | custom-call | tf_op jit(solution)/shard_map/exchange/pallas_call | solution.py:343
  19.6 3.0 %finish.1 = (f32[16,3,32,1024]{3,2,1,0:T(8,128)}, f32[3,32,1024]{2,1,0:T(8,128)}) custom-call(f32[8,3,32,1024]{3,2,1,0:T(8,128)S(1)} %get-tuple-element.12.base, f32[8,3,32,1024]{3,2,1,0:T(8,128)S(1)} %get-tuple-element.13.slope, f32[4,8,3,8,128]{4,3,2,1,0:T(8,128)S(1)} %get-tuple-element.14.squares, f32[3,32,1024]{2,1,0:T(8,128)S(1)} %get-tuple-element.15.quiet, ...), custom_call_target="tpu_custom_call" | custom-call | tf_op jit(solution)/shard_map/finish/pallas_call | solution.py:378

commit v5 on v4

--- a/solution.py
+++ b/solution.py
@@ -16,7 +16,7 @@
 HALF = TILES // 2
 SUB, GROUPS = 8, 4
 PIECES = (3, 0, 1, 2)
-ROUTES = ("x", "direct", "direct", "y")
+ROUTES = ("x", "x", "direct", "y")
 PEERS = ((2, 1), (1, 1), (3, 1), (2, 0), (0, 1), (1, 0), (3, 0))
 
 

time: 22.6 us -> 22.5 us (level)
  no operation moved by 1% of the time
where the time goes in v5:
time: 22.5 us; the launch traced here: 22.4 us
  Pallas kernels  21.8 us (97%)
  between operations  0.64 us (3%)
    pallas_call x1, Pallas kernels, shards(): pl.pallas_call(exchange, out_shape=[pltpu.VMEM(shape, F32) for shape in h...  18.8 us
    pallas_call x1, Pallas kernels, shards(): pl.pallas_call(finish, out_shape=[jax.ShapeDtypeStruct(order.shape, F32),...  2.98 us

profile of v5, /device:TPU:2, one launch (start us, length us, event | category | flops | bytes accessed | tf_op | source)
XLA Modules:
  0.0 22.4 jit_solution(16074487905646121068)
XLA Ops:
  0.6 18.8 %exchange.1 = (f32[8,3,32,1024]{3,2,1,0:T(8,128)S(1)}, f32[8,3,32,1024]{3,2,1,0:T(8,128)S(1)}, f32[4,8,3,8,128]{4,3,2,1,0:T(8,128)S(1)}, f32[3,32,1024]{2,1,0:T(...) custom-call(f32[16,3,32,1024]{3,2,1,0:T(8,128)} %order.1, ...), custom_call_target="tpu_custom_call" | custom-call | tf_op jit(solution)/shard_map/exchange/pallas_call | solution.py:343
  19.5 3.0 %finish.1 = (f32[16,3,32,1024]{3,2,1,0:T(8,128)}, f32[3,32,1024]{2,1,0:T(8,128)}) custom-call(f32[8,3,32,1024]{3,2,1,0:T(8,128)S(1)} %get-tuple-element.12.base, f32[8,3,32,1024]{3,2,1,0:T(8,128)S(1)} %get-tuple-element.13.slope, f32[4,8,3,8,128]{4,3,2,1,0:T(8,128)S(1)} %get-tuple-element.14.squares, f32[3,32,1024]{2,1,0:T(8,128)S(1)} %get-tuple-element.15.quiet, ...), custom_call_target="tpu_custom_call" | custom-call | tf_op jit(solution)/shard_map/finish/pallas_call | solution.py:378
